TPU v7x, 32 devices: a whole 2x2x4 slice. The times are simulated.
32 devices in a mesh: dp: 2 (over y), ctx: 16 (over z, x, core).
Axes of the slice: x: 2, y: 2, z: 4, core: 2. Of those that a mesh axis runs over, the one named last changes fastest.
Arguments:
- tokens: bfloat16 [8192, 1024], P(('dp', 'ctx')), may hold values from -6 to 6
- seq_lengths: int32 [2, 4], P('dp'), may hold values from 1 to 2048, 4096 in all within a row
- dealing: int32 [2, 64], P('dp'), may hold values from 0 to 63, as said below
- ln1_gain: bfloat16 [1024], P(('dp', 'ctx')), may hold values from 0.5 to 1.5
- ln1_bias: bfloat16 [1024], P(('dp', 'ctx')), may hold values from -1 to 1
- ln2_gain: bfloat16 [1024], P(('dp', 'ctx')), may hold values from 0.5 to 1.5
- ln2_bias: bfloat16 [1024], P(('dp', 'ctx')), may hold values from -1 to 1
- w_qkv: bfloat16 [1024, 3072], P(('dp', 'ctx')), may hold values from -0.25 to 0.25
- b_qkv: bfloat16 [3072], P(('dp', 'ctx')), may hold values from -1 to 1
- w_out: bfloat16 [1024, 1024], P(('dp', 'ctx')), may hold values from -0.75 to 0.75
- w_in: bfloat16 [1024, 4096], P(('dp', 'ctx')), may hold values from -0.1875 to 0.1875
- b_in: bfloat16 [4096], P(('dp', 'ctx')), may hold values from -2.5 to 2.5
- w_fc2: bfloat16 [4096, 1024], P(('dp', 'ctx')), may hold values from -0.09375 to 0.09375
- b_out: bfloat16 [1024], P(('dp', 'ctx')), may hold values from -1 to 1
- cotangent: bfloat16 [8192, 1024], P(('dp', 'ctx')), may hold values from -6 to 6
Outputs:
- mixed: bfloat16 [8192, 1024], P(('dp', 'ctx'))
- grad_tokens: float32 [8192, 1024], P(('dp', 'ctx'))
- grad_ln1_gain: float32 [1024], P(('dp', 'ctx'))
- grad_ln1_bias: float32 [1024], P(('dp', 'ctx'))
- grad_ln2_gain: float32 [1024], P(('dp', 'ctx'))
- grad_ln2_bias: float32 [1024], P(('dp', 'ctx'))
- grad_w_qkv: float32 [1024, 3072], P(('dp', 'ctx'))
- grad_b_qkv: float32 [3072], P(('dp', 'ctx'))
- grad_w_out: float32 [1024, 1024], P(('dp', 'ctx'))
- grad_w_in: float32 [1024, 4096], P(('dp', 'ctx'))
- grad_b_in: float32 [4096], P(('dp', 'ctx'))
- grad_w_fc2: float32 [4096, 1024], P(('dp', 'ctx'))
- grad_b_out: float32 [1024], P(('dp', 'ctx'))
Inputs may be any that keep to these rules, and one draw needn't show every extreme that they name: `seq_lengths`: each row gives, in order, the lengths of the sequences packed into the 4096 places of one group; a row sums to 4096; its largest is exactly 2048. `dealing`: each row names every packed block of 64 places once. Slots are ordered by ctx index and then by local block; the slots at one local place b of all ctx indices hold, in some order, one run of consecutive packed blocks that starts at b times the number of ctx devices.
All inputs are finite; a program needn't handle non-finite values.
Results may differ from a plain program's by a relative error of at most 0.012.
The roundings to bfloat16 on the way count: a program that leaves them out, or rounds other values in their place, can miss the bound.
Values may be sent and summed in bfloat16 or wider, within the bound.
No kernel may reach another device: no remote copies, remote signals or barrier semaphores. Data moves between devices by JAX's collectives and lax.ppermute only.
A program may use at most 320 MiB of HBM per device.

v0:
```python
import jax
import jax.numpy as jnp
from jax import lax
from jax.sharding import PartitionSpec as P

HEAD = 64
ROT = 16
LONGEST = 2048


epsilon = 1e-05
neg_big = -1e30


def layer_norm(values, gain, shift):
    centre = jnp.mean(values, axis=-1, keepdims=True)
    centred = values - centre
    spread = jnp.mean(centred * centred, axis=-1, keepdims=True)
    return centred * lax.rsqrt(spread + epsilon) * gain + shift


def exact_gelu(values):
    return jax.nn.gelu(values, approximate=False)


def angles(position, rotary):
    half = rotary // 2
    freq = 10000.0 ** (-2.0 * jnp.arange(half, dtype=jnp.float32) / rotary)
    phase = position.astype(jnp.float32)[:, None] * freq[None, :]
    return (jnp.cos(phase), jnp.sin(phase))


def rotate(heads_in, cosine, sine):
    half = cosine.shape[-1]
    first = heads_in[..., :half]
    second = heads_in[..., half : 2 * half]
    cos_b = cosine[:, None, :]
    sin_b = sine[:, None, :]
    return jnp.concatenate(
        [first * cos_b - second * sin_b, second * cos_b + first * sin_b, heads_in[..., 2 * half :]],
        axis=-1,
    )


def token_meta(lengths, order, rows, block):
    slot_count = order.shape[0]
    owner = rows // block
    picked = jnp.sum(
        jnp.where(
            owner[:, None] == jnp.arange(slot_count, dtype=jnp.int32)[None, :], order[None, :], 0
        ),
        axis=1,
    )
    packed = picked * block + rows % block
    ends = jnp.cumsum(lengths)
    document = jnp.sum((packed[:, None] >= ends[None, :]).astype(jnp.int32), axis=1)
    starts = ends - lengths
    seq_count = lengths.shape[0]
    first = jnp.sum(
        jnp.where(
            document[:, None] == jnp.arange(seq_count, dtype=jnp.int32)[None, :], starts[None, :], 0
        ),
        axis=1,
    )
    return (document, packed - first)


def body(
    tokens,
    seq_lengths,
    dealing,
    ln1_gain,
    ln1_bias,
    ln2_gain,
    ln2_bias,
    w_qkv,
    b_qkv,
    w_out,
    w_in,
    b_in,
    w_fc2,
    b_out,
    cotangent,
):
    shard_count = lax.axis_size("ctx")
    rows_dev, width = tokens.shape
    block = LONGEST // (2 * shard_count)
    heads = width // HEAD
    scale = HEAD ** (-0.5)
    lengths = seq_lengths[0]
    order = dealing[0]
    own_rows = lax.axis_index("ctx") * rows_dev + jnp.arange(rows_dev, dtype=jnp.int32)
    doc_query, pos_query = token_meta(lengths, order, own_rows, block)
    cosine, sine = angles(pos_query, ROT)
    gathered = (
        lax.all_gather(ln1_gain, ("dp", "ctx"), axis=0, tiled=True),
        lax.all_gather(ln1_bias, ("dp", "ctx"), axis=0, tiled=True),
        lax.all_gather(ln2_gain, ("dp", "ctx"), axis=0, tiled=True),
        lax.all_gather(ln2_bias, ("dp", "ctx"), axis=0, tiled=True),
        lax.all_gather(w_qkv, ("dp", "ctx"), axis=0, tiled=True),
        lax.all_gather(b_qkv, ("dp", "ctx"), axis=0, tiled=True),
        lax.all_gather(w_out, ("dp", "ctx"), axis=0, tiled=True),
        lax.all_gather(w_in, ("dp", "ctx"), axis=0, tiled=True),
        lax.all_gather(b_in, ("dp", "ctx"), axis=0, tiled=True),
        lax.all_gather(w_fc2, ("dp", "ctx"), axis=0, tiled=True),
        lax.all_gather(b_out, ("dp", "ctx"), axis=0, tiled=True),
    )
    (
        gain_one,
        shift_one,
        gain_two,
        shift_two,
        weight_qkv,
        bias_qkv,
        weight_out,
        weight_in,
        bias_in,
        weight_fc2,
        bias_out,
    ) = gathered
    inputs = tokens.astype(jnp.float32)
    norm_one, back_one = jax.vjp(
        layer_norm, inputs, gain_one.astype(jnp.float32), shift_one.astype(jnp.float32)
    )
    norm_two, back_two = jax.vjp(
        layer_norm, inputs, gain_two.astype(jnp.float32), shift_two.astype(jnp.float32)
    )
    low_one = norm_one.astype(jnp.bfloat16)
    low_two = norm_two.astype(jnp.bfloat16)
    joined = jnp.dot(low_one, weight_qkv, preferred_element_type=jnp.float32) + bias_qkv.astype(
        jnp.float32
    )
    query_raw = joined[:, :width].reshape(rows_dev, heads, HEAD)
    key_raw = joined[:, width : 2 * width].reshape(rows_dev, heads, HEAD)
    query_rot, back_rotate = jax.vjp(lambda heads_in: rotate(heads_in, cosine, sine), query_raw)
    key_rot = rotate(key_raw, cosine, sine)
    query = query_rot.astype(jnp.bfloat16)
    key_value = jnp.concatenate(
        [key_rot.reshape(rows_dev, width), joined[:, 2 * width :]], axis=1
    ).astype(jnp.bfloat16)

    def piece_scores(piece):
        count = piece.shape[0]
        doc_key, pos_key = token_meta(lengths, order, jnp.arange(count, dtype=jnp.int32), block)
        keys = piece[:, :width].reshape(count, heads, HEAD)
        values = piece[:, width:].reshape(count, heads, HEAD)
        score = jnp.einsum("qhd,khd->hqk", query, keys, preferred_element_type=jnp.float32) * scale
        allowed = (
            (doc_query[:, None] == doc_key[None, :]) & (pos_key[None, :] <= pos_query[:, None])
        )[None]
        return (keys, values, jnp.where(allowed, score, neg_big), allowed)

    row_top = jnp.full((heads, rows_dev), neg_big, jnp.float32)
    keys, values, score, allowed = piece_scores(
        lax.all_gather(key_value, "ctx", axis=0, tiled=True)
    )
    new_top = jnp.maximum(row_top, jnp.max(score, axis=-1))
    weight = jnp.where(allowed, jnp.exp(score - new_top[..., None]), 0.0)
    row_total = jnp.sum(weight, axis=-1)
    part_sum = jnp.einsum(
        "hqk,khd->qhd", weight.astype(jnp.bfloat16), values, preferred_element_type=jnp.float32
    )
    accum = part_sum
    row_top, row_total, accum = (new_top, row_total, accum)
    attended = accum / jnp.transpose(row_total)[:, :, None]
    log_sum = row_top + jnp.log(row_total)
    attended_low = attended.reshape(rows_dev, width).astype(jnp.bfloat16)
    up_in = jnp.dot(low_two, weight_in, preferred_element_type=jnp.float32) + bias_in.astype(
        jnp.float32
    )
    hidden, back_gelu = jax.vjp(exact_gelu, up_in)
    hidden_low = hidden.astype(jnp.bfloat16)
    result = (
        inputs
        + jnp.dot(attended_low, weight_out, preferred_element_type=jnp.float32)
        + jnp.dot(hidden_low, weight_fc2, preferred_element_type=jnp.float32)
        + bias_out.astype(jnp.float32)
    )
    mixed = result.astype(jnp.bfloat16)
    back_qkv, back_out, back_in, back_fc2 = (
        lax.all_gather(w_qkv, ("dp", "ctx"), axis=0, tiled=True),
        lax.all_gather(w_out, ("dp", "ctx"), axis=0, tiled=True),
        lax.all_gather(w_in, ("dp", "ctx"), axis=0, tiled=True),
        lax.all_gather(w_fc2, ("dp", "ctx"), axis=0, tiled=True),
    )
    grad_result = cotangent.astype(jnp.float32)
    grad_bias_out = jnp.sum(grad_result, axis=0)
    grad_weight_fc2 = jnp.dot(hidden_low.T, cotangent, preferred_element_type=jnp.float32)
    grad_hidden = jnp.dot(cotangent, back_fc2.T, preferred_element_type=jnp.float32)
    grad_up = back_gelu(grad_hidden)[0].astype(jnp.bfloat16)
    grad_weight_in = jnp.dot(low_two.T, grad_up, preferred_element_type=jnp.float32)
    grad_bias_in = jnp.sum(grad_up.astype(jnp.float32), axis=0)
    grad_norm_two = jnp.dot(grad_up, back_in.T, preferred_element_type=jnp.float32)
    grad_weight_out = jnp.dot(attended_low.T, cotangent, preferred_element_type=jnp.float32)
    grad_attended = (
        jnp.dot(cotangent, back_out.T, preferred_element_type=jnp.float32)
        .astype(jnp.bfloat16)
        .reshape(rows_dev, heads, HEAD)
    )
    delta = jnp.transpose(jnp.sum(grad_attended.astype(jnp.float32) * attended, axis=-1))
    piece = lax.all_gather(key_value, "ctx", axis=0, tiled=True)
    count = piece.shape[0]
    keys, values, score, allowed = piece_scores(piece)
    prob = jnp.where(allowed, jnp.exp(score - log_sum[..., None]), 0.0)
    grad_values = jnp.einsum(
        "hqk,qhd->khd", prob.astype(jnp.bfloat16), grad_attended, preferred_element_type=jnp.float32
    )
    grad_prob = jnp.einsum(
        "qhd,khd->hqk", grad_attended, values, preferred_element_type=jnp.float32
    )
    grad_score = (prob * (grad_prob - delta[..., None])).astype(jnp.bfloat16)
    grad_query = (
        jnp.einsum("hqk,khd->qhd", grad_score, keys, preferred_element_type=jnp.float32) * scale
    )
    grad_keys = (
        jnp.einsum("hqk,qhd->khd", grad_score, query, preferred_element_type=jnp.float32) * scale
    )
    update = jnp.concatenate(
        [grad_keys.reshape(count, width), grad_values.reshape(count, width)], axis=1
    )
    grad_pairs = update
    folded = (grad_query, grad_pairs)
    grad_query, grad_pairs = folded
    grad_own = lax.psum_scatter(
        grad_pairs.astype(jnp.bfloat16), "ctx", scatter_dimension=0, tiled=True
    ).astype(jnp.float32)
    grad_key_rot = grad_own[:, :width].reshape(rows_dev, heads, HEAD)
    grad_joined = jnp.concatenate(
        [
            back_rotate(grad_query)[0].reshape(rows_dev, width),
            back_rotate(grad_key_rot)[0].reshape(rows_dev, width),
            grad_own[:, width:],
        ],
        axis=1,
    ).astype(jnp.bfloat16)
    grad_weight_qkv = jnp.dot(low_one.T, grad_joined, preferred_element_type=jnp.float32)
    grad_bias_qkv = jnp.sum(grad_joined.astype(jnp.float32), axis=0)
    grad_norm_one = jnp.dot(grad_joined, back_qkv.T, preferred_element_type=jnp.float32)
    grad_in_one, grad_gain_one, grad_shift_one = back_one(grad_norm_one)
    grad_in_two, grad_gain_two, grad_shift_two = back_two(grad_norm_two)
    grad_inputs = grad_result + grad_in_one + grad_in_two
    reduced = (
        lax.psum_scatter(grad_gain_one, ("dp", "ctx"), scatter_dimension=0, tiled=True),
        lax.psum_scatter(grad_shift_one, ("dp", "ctx"), scatter_dimension=0, tiled=True),
        lax.psum_scatter(grad_gain_two, ("dp", "ctx"), scatter_dimension=0, tiled=True),
        lax.psum_scatter(grad_shift_two, ("dp", "ctx"), scatter_dimension=0, tiled=True),
        lax.psum_scatter(grad_weight_qkv, ("dp", "ctx"), scatter_dimension=0, tiled=True),
        lax.psum_scatter(grad_bias_qkv, ("dp", "ctx"), scatter_dimension=0, tiled=True),
        lax.psum_scatter(grad_weight_out, ("dp", "ctx"), scatter_dimension=0, tiled=True),
        lax.psum_scatter(grad_weight_in, ("dp", "ctx"), scatter_dimension=0, tiled=True),
        lax.psum_scatter(grad_bias_in, ("dp", "ctx"), scatter_dimension=0, tiled=True),
        lax.psum_scatter(grad_weight_fc2, ("dp", "ctx"), scatter_dimension=0, tiled=True),
        lax.psum_scatter(grad_bias_out, ("dp", "ctx"), scatter_dimension=0, tiled=True),
    )
    return (
        mixed,
        grad_inputs,
        reduced[0],
        reduced[1],
        reduced[2],
        reduced[3],
        reduced[4],
        reduced[5],
        reduced[6],
        reduced[7],
        reduced[8],
        reduced[9],
        reduced[10],
    )


def solution(mesh):
    placed = (
        P(("dp", "ctx"), None),
        P("dp", None),
        P("dp", None),
        P(("dp", "ctx")),
        P(("dp", "ctx")),
        P(("dp", "ctx")),
        P(("dp", "ctx")),
        P(("dp", "ctx"), None),
        P(("dp", "ctx")),
        P(("dp", "ctx"), None),
        P(("dp", "ctx"), None),
        P(("dp", "ctx")),
        P(("dp", "ctx"), None),
        P(("dp", "ctx")),
        P(("dp", "ctx"), None),
    )
    return jax.shard_map(
        body,
        mesh=mesh,
        in_specs=placed,
        out_specs=(
            P(("dp", "ctx"), None),
            P(("dp", "ctx"), None),
            P(("dp", "ctx")),
            P(("dp", "ctx")),
            P(("dp", "ctx")),
            P(("dp", "ctx")),
            P(("dp", "ctx"), None),
            P(("dp", "ctx")),
            P(("dp", "ctx"), None),
            P(("dp", "ctx"), None),
            P(("dp", "ctx")),
            P(("dp", "ctx"), None),
            P(("dp", "ctx")),
        ),
        check_vma=False,
    )
```

profile of v0, /device:TPU:0, one launch (start us, length us, event | category | flops | bytes accessed | tf_op | source)
XLA Modules:
  0.0 1345.6 jit_solution(8746638571451892862)
XLA Ops:
  13.8 42.4 %all-reduce.20 = (bf16[1024]{0:T(1024)(128)(2,1)}, bf16[1024]{0:T(1024)(128)(2,1)}, bf16[3072]{0:T(1024)(128)(2,1)S(1)}, bf16[1024]{0:T(1024)(128)(2,1)S(1)}, bf...) all-reduce(bf16[1024]{0:T(1024)(128)(2,1)S(1)} %dynamic-update-slic, ...), channel_id=1, replica_groups=mesh['dp'=2,'ctx'=16] {'dp','ctx'}, use_global_device_ids=true, to_apply=%add.10 | all-reduce | flops 8192 | bytes 32768
  62.1 21.0 %all-gather.7.cloned.1.call-done = bf16[1024,3072]{1,0:T(8,128)(2,1)} async-done(((bf16[32,3072]{1,0:T(8,128)(2,1)}), bf16[1024,3072]{1,0:T(8,128)(2,1)}) %all-gather.7.cloned.1.call-update) | async-done | bytes 6291472 | tf_op jit(solution)/shard_map/all_gather | solution.py:100
  99.6 41.5 %all-gather.11.cloned.1.call-done = bf16[1024,1024]{1,0:T(8,128)(2,1)} async-done(((bf16[32,1024]{1,0:T(8,128)(2,1)}), bf16[1024,1024]{1,0:T(8,128)(2,1)}) %all-gather.11.cloned.1.call-update) | async-done | bytes 2097168 | tf_op jit(solution)/shard_map/all_gather | solution.py:102
  143.7 125.9 %all-gather.9.cloned.1.call-done = bf16[4096,2048]{1,0:T(8,128)(2,1)} async-done(((bf16[256,2048]{1,0:T(8,128)(2,1)}), bf16[4096,2048]{1,0:T(8,128)(2,1)}) %all-gather.9.cloned.1.call-update) | async-done | bytes 16777232 | tf_op jit(solution)/shard_map/all_gather | solution.py:155
  269.6 12.1 fusion.80
  281.7 11.4 copy.56
  293.1 28.8 %fusion.83 = (f32[16,256]{1,0:T(8,128)S(1)}, f32[16,256,4096]{2,1,0:T(8,128)}) fusion(bf16[4096,16,64]{0,2,1:T(8,128)(2,1)} %bitcast.63, bf16[256,16,48]{0,2,1:T(8,128)(2,1)S(1)} %slice.84, bf16[256,16,8]{0,2,1:T(8,128)(2,1)S(1)} %copy-done.15, bf16[256,16,8]{0,2,1:T(8,128)(2,1)S(1)} %copy-done.14, pred[256,4096]{1,0:T(8,128)(4,1)S(1)} %compare_and_fusion), kind=kOutput, calls=%fused_computation.153 | convolution fusion | flops 2199384064 | bytes 77086720 | tf_op jit(solution)/shard_map/qhd,khd->hqk/dot_general | solution.py:147
  321.9 22.0 %fusion = f32[16,256]{1,0:T(8,128)S(1)} fusion(f32[16,256,4096]{2,1,0:T(8,128)} %get-tuple-element.70, f32[16,256]{1,0:T(8,128)S(1)} %broadcast_maximum_fusion, pred[256,4096]{1,0:T(8,128)(4,1)S(1)} %compare_and_fusion), kind=kLoop, calls=%fused_computation.4 | loop fusion | flops 50327552 | bytes 68190208 | tf_op jit(solution)/shard_map/reduce_sum | solution.py:159
  343.9 11.4 copy.54
  355.3 27.3 %multiply_reduce_fusion = (f32[256,16]{0,1:T(8,128)S(1)}, bf16[256,16,64]{0,2,1:T(8,128)(2,1)}) fusion(bf16[256,1024]{0,1:T(8,128)(2,1)S(1)} %copy.57, f32[256,16]{0,1:T(8,128)S(1)} %bitcast.86, bf16[4096,16,64]{0,2,1:T(8,128)(2,1)} %bitcast.67, f32[16,256,4096]{2,1,0:T(8,128)} %get-tuple-element.70, f32[16,256]{1,0:T(8,128)S(1)} %broadcast_maximum_fusion, ...), kind=kOutput, calls=%fused_computation.78 | convolution fusion | flops 2199121920 | bytes 77643776 | tf_op jit(solution)/shard_map/hqk,khd->qhd/dot_general | solution.py:160
  382.6 42.4 %multiply_convert_fusion = bf16[16,256,4096]{2,1,0:T(8,128)(2,1)} fusion(f32[16,256,4096]{2,1,0:T(8,128)} %get-tuple-element.70, bf16[256,16,64]{0,2,1:T(8,128)(2,1)S(1)} %bitcast.79, bf16[4096,16,64]{0,2,1:T(8,128)(2,1)} %bitcast.68, f32[16,256]{1,0:T(8,128)S(1)} %bitcast.96, f32[16,256]{1,0:T(8,128)S(1)} %log_add_fusion, ...), kind=kOutput, calls=%fused_computation | convolution fusion | flops 2231369728 | bytes 110657536 | tf_op jit(solution)/shard_map/qhd,khd->hqk/dot_general | solution.py:208
  425.0 17.3 %multiply_convert_fusion.1 = bf16[16,64,4096]{2,1,0:T(8,128)(2,1)} fusion(bf16[16,256,4096]{2,1,0:T(8,128)(2,1)} %multiply_convert_fusion, bf16[256,16,48]{0,2,1:T(8,128)(2,1)S(1)} %slice.84, bf16[256,16,8]{0,2,1:T(8,128)(2,1)S(1)} %copy-done.15, bf16[256,16,8]{0,2,1:T(8,128)(2,1)S(1)} %copy-done.14), kind=kOutput, calls=%fused_computation.14 | convolution fusion | flops 2157445120 | bytes 42467328 | tf_op jit(solution)/shard_map/hqk,qhd->khd/dot_general | solution.py:216
  442.3 27.9 %fusion.11 = bf16[16,64,4096]{2,1,0:T(8,128)(2,1)} fusion(bf16[256,16,64]{0,2,1:T(8,128)(2,1)S(1)} %bitcast.80, f32[16,256,4096]{2,1,0:T(8,128)} %get-tuple-element.70, f32[16,256]{1,0:T(8,128)S(1)} %log_add_fusion, pred[256,4096]{1,0:T(8,128)(4,1)S(1)} %compare_and_fusion), kind=kOutput, calls=%fused_computation.15 | convolution fusion | flops 2202009600 | bytes 77086720 | tf_op jit(solution)/shard_map/hqk,qhd->khd/dot_general | solution.py:205
  470.2 13.7 %pad_maximum_fusion = bf16[4096,2048]{0,1:T(8,128)(2,1)} fusion(bf16[4096,1024]{0,1:T(8,128)(2,1)} %bitcast.65, bf16[4096,1024]{0,1:T(8,128)(2,1)} %bitcast.66), kind=kLoop, calls=%fused_computation.13 | loop fusion | flops 33554432 | bytes 33554432 | tf_op jit(solution)/shard_map/concatenate | solution.py:218
  484.6 38.8 %all-gather = bf16[32,1,128]{2,1,0:T(2,128)(2,1)S(1)} all-gather(bf16[1,1,128]{2,1,0:T(2,128)(2,1)S(1)} %bitcast.92), channel_id=1, replica_groups=mesh['dp'=2,'ctx'=16] {'dp','ctx'}, dimensions={0}, use_global_device_ids=true | all-gather | bytes 8448 | tf_op jit(solution)/shard_map/all_gather | solution.py:104
  531.4 16.2 %convert_reduce_fusion = (f32[4096]{0:T(1024)S(1)}, bf16[256,4096]{1,0:T(8,128)(2,1)}, f32[256,4096]{1,0:T(8,128)S(1)}) fusion(f32[256,4096]{1,0:T(8,128)} %convolution_add_fusion, bf16[256,1024]{1,0:T(8,128)(2,1)S(1)} %copy-done.9, bf16[4096,1024]{1,0:T(8,128)(2,1)} %all-gather.15.cloned.1.call-done), kind=kOutput, calls=%fused_computation.19 | convolution fusion | flops 2225074176 | bytes 19415040 | tf_op jit(solution)/shard_map/dot_general | solution.py:189
  556.8 9.8 fusion.67
  570.5 18.8 %fusion.30 = f32[256,16,64]{0,2,1:T(8,128)} fusion(bf16[4096,16,64]{0,2,1:T(8,128)(2,1)} %bitcast.64, bf16[16,256,4096]{2,1,0:T(8,128)(2,1)} %multiply_convert_fusion), kind=kOutput, calls=%fused_computation.55 | convolution fusion | flops 2147745792 | bytes 42991616 | tf_op jit(solution)/shard_map/hqk,khd->qhd/dot_general | solution.py:213
  589.4 72.1 %reduce-scatter.6.cloned.1.call-done = bf16[256,2048]{0,1:T(8,128)(2,1)} async-done(((bf16[4096,2048]{0,1:T(8,128)(2,1)}), bf16[256,2048]{0,1:T(8,128)(2,1)}) %reduce-scatter.6.cloned.1.call-update) | async-done | bytes 1048592 | tf_op jit(solution)/shard_map/reduce_scatter | solution.py:224
  691.3 46.1 %all-reduce.19 = (f32[1024]{0:T(1024)S(1)}, f32[1024]{0:T(1024)S(1)}, f32[1024]{0:T(1024)S(1)}, f32[1024]{0:T(1024)S(1)}, f32[3072]{0:T(1024)S(1)}, /*index=5*/f32[4096]{0:T(1024)S(1)}, f32[1024]{0:T(1024)S(1)}) all-reduce(f32[1024]{0:T(1024)S(1)} %get-tuple-element.22, ...), channel_id=3, replica_groups=mesh['dp'=2,'ctx'=16] {'dp','ctx'}, use_global_device_ids=true, to_apply=%region_18.19.clone | all-reduce | flops 12288 | bytes 98304
  741.5 103.5 %reduce-scatter.14.cloned.1.call-done = f32[128,1024]{1,0:T(8,128)} async-done(((f32[4096,1024]{1,0:T(8,128)}), f32[128,1024]{1,0:T(8,128)}) %reduce-scatter.14.cloned.1.call-update) | async-done | bytes 524304 | tf_op jit(solution)/shard_map/reduce_scatter | solution.py:252
  845.0 187.3 %reduce-scatter.12.cloned.1.call-done = f32[32,4096]{1,0:T(8,128)} async-done(((f32[1024,4096]{1,0:T(8,128)}), f32[32,4096]{1,0:T(8,128)}) %reduce-scatter.12.cloned.1.call-update) | async-done | bytes 524304 | tf_op jit(solution)/shard_map/reduce_scatter | solution.py:250
  1032.4 147.4 %reduce-scatter.10.cloned.1.call-done = f32[32,1024]{1,0:T(8,128)} async-done(((f32[1024,1024]{1,0:T(8,128)}), f32[32,1024]{1,0:T(8,128)}) %reduce-scatter.10.cloned.1.call-update) | async-done | bytes 131088 | tf_op jit(solution)/shard_map/reduce_scatter | solution.py:249
  1179.7 158.6 %reduce-scatter.8.cloned.1.call-done = f32[32,3072]{1,0:T(8,128)} async-done(((f32[1024,3072]{1,0:T(8,128)}), f32[32,3072]{1,0:T(8,128)}) %reduce-scatter.8.cloned.1.call-update) | async-done | bytes 393232 | tf_op jit(solution)/shard_map/reduce_scatter | solution.py:247
  (186 shorter events, 86.5 us)
Async XLA Ops:
  7.2 76.0 %all-gather.7.cloned.1.call-start = ((), (), s32[]{:S(2)}) async-start(), calls=%async_computation.5 | async-start | bytes 6488064 | tf_op jit(solution)/shard_map/all_gather | solution.py:100
  7.9 133.2 %all-gather.11.cloned.1.call-start = ((), (), s32[]{:S(2)}) async-start(), calls=%async_computation.7 | async-start | bytes 2162688 | tf_op jit(solution)/shard_map/all_gather | solution.py:102
  8.7 260.9 %all-gather.9.cloned.1.call-start = ((), (), s32[]{:S(2)}) async-start(), calls=%async_computation.6 | async-start | bytes 17825792 | tf_op jit(solution)/shard_map/all_gather | solution.py:155
  56.2 31.9 %copy-start.16 = (f32[1024]{0:T(1024)}, f32[1024]{0:T(1024)S(1)}, u32[]{:S(2)}) copy-start(f32[1024]{0:T(1024)S(1)} %convert_element_type.89) | copy-start | bytes 12292
  56.2 31.9 %copy-start.18 = (f32[1024]{0:T(1024)}, f32[1024]{0:T(1024)S(1)}, u32[]{:S(2)}) copy-start(f32[1024]{0:T(1024)S(1)} %convert_element_type.90) | copy-start | bytes 12292
  57.1 31.0 %copy-start.31 = (s32[4,1]{0,1:T(1,128)}, s32[4,1]{0,1:T(1,128)S(1)}, u32[]{:S(2)}) copy-start(s32[4,1]{0,1:T(1,128)S(1)} %reduce-window.4) | copy-start | bytes 52
  60.0 28.1 %copy-start.20 = (f32[256]{0:T(256)}, f32[256]{0:T(256)S(1)}, u32[]{:S(2)}) copy-start(f32[256]{0:T(256)S(1)} %broadcast_multiply_fusion) | copy-start | bytes 3076
  61.4 26.7 %copy-start.22 = (f32[256]{0:T(256)}, f32[256]{0:T(256)S(1)}, u32[]{:S(2)}) copy-start(f32[256]{0:T(256)S(1)} %fusion.60) | copy-start | bytes 3076
  62.1 29.1 %copy-start.24 = (f32[256,8]{0,1:T(8,128)}, f32[256,8]{0,1:T(8,128)S(1)}, u32[]{:S(2)}) copy-start(f32[256,8]{0,1:T(8,128)S(1)} %get-tuple-element.67) | copy-start | bytes 24580
  62.1 29.1 %copy-start.26 = (f32[256,8]{0,1:T(8,128)}, f32[256,8]{0,1:T(8,128)S(1)}, u32[]{:S(2)}) copy-start(f32[256,8]{0,1:T(8,128)S(1)} %get-tuple-element.68) | copy-start | bytes 24580
  90.0 51.1 %copy-start.8 = (bf16[256,1024]{1,0:T(8,128)(2,1)S(1)}, bf16[256,1024]{1,0:T(8,128)(2,1)}, u32[]{:S(2)}) copy-start(bf16[256,1024]{1,0:T(8,128)(2,1)} %param.29) | copy-start | bytes 1572868
  94.3 429.1 %all-gather.13.cloned.1.call-start = ((), (), s32[]{:S(2)}) async-start(), calls=%async_computation.8 | async-start | bytes 8650752 | tf_op jit(solution)/shard_map/all_gather | solution.py:103
  94.9 436.5 %all-gather.15.cloned.1.call-start = ((), (), s32[]{:S(2)}) async-start(), calls=%async_computation.9 | async-start | bytes 8650752 | tf_op jit(solution)/shard_map/all_gather | solution.py:105
  95.5 566.0 %reduce-scatter.6.cloned.1.call-start = ((), (), s32[]{:S(2)}) async-start(), calls=%async_computation.10 | async-start | bytes 17825792 | tf_op jit(solution)/shard_map/reduce_scatter | solution.py:224
  483.9 39.5 %copy-start = (bf16[256,1024]{1,0:T(8,128)(2,1)S(1)}, bf16[256,1024]{1,0:T(8,128)(2,1)}, u32[]{:S(2)}) copy-start(bf16[256,1024]{1,0:T(8,128)(2,1)} %param.15) | copy-start | bytes 1572868
  483.9 39.5 %copy-start.21 = (f32[256]{0:T(256)S(1)}, f32[256]{0:T(256)}, u32[]{:S(2)}) copy-start(f32[256]{0:T(256)} %copy-done.20) | copy-start | bytes 3076
  483.9 39.5 %copy-start.23 = (f32[256]{0:T(256)S(1)}, f32[256]{0:T(256)}, u32[]{:S(2)}) copy-start(f32[256]{0:T(256)} %copy-done.22) | copy-start | bytes 3076
  483.9 361.1 %reduce-scatter.14.cloned.1.call-start = ((), (), s32[]{:S(2)}) async-start(), calls=%async_computation.14 | async-start | bytes 17301504 | tf_op jit(solution)/shard_map/reduce_scatter | solution.py:252
  556.7 475.7 %reduce-scatter.12.cloned.1.call-start = ((), (), s32[]{:S(2)}) async-start(), calls=%async_computation.13 | async-start | bytes 17301504 | tf_op jit(solution)/shard_map/reduce_scatter | solution.py:250
  566.6 613.1 %reduce-scatter.10.cloned.1.call-start = ((), (), s32[]{:S(2)}) async-start(), calls=%async_computation.12 | async-start | bytes 4325376 | tf_op jit(solution)/shard_map/reduce_scatter | solution.py:249
  570.5 767.9 %reduce-scatter.8.cloned.1.call-start = ((), (), s32[]{:S(2)}) async-start(), calls=%async_computation.11 | async-start | bytes 12976128 | tf_op jit(solution)/shard_map/reduce_scatter | solution.py:247
  589.4 73.7 %copy-start.25 = (f32[256,8]{0,1:T(8,128)S(1)}, f32[256,8]{0,1:T(8,128)}, u32[]{:S(2)}) copy-start(f32[256,8]{0,1:T(8,128)} %copy-done.24) | copy-start | bytes 24580
  589.4 73.7 %copy-start.27 = (f32[256,8]{0,1:T(8,128)S(1)}, f32[256,8]{0,1:T(8,128)}, u32[]{:S(2)}) copy-start(f32[256,8]{0,1:T(8,128)} %copy-done.26) | copy-start | bytes 24580
  589.4 73.8 %slice-start = ((f32[256,16,64]{0,2,1:T(8,128)}), f32[256,16,48]{0,2,1:T(8,128)S(1)}, s32[]{:S(2)}) async-start(f32[256,16,64]{0,2,1:T(8,128)} %fusion.30), calls=%async_computation.15 | async-start | bytes 1572864 | tf_op jit(solution)/shard_map/transpose(jvp())/split | solution.py:39
  (26 other events, 104.7 us)
Sparse Core Ops, SparseCore 0:
  10.9 72.2 all-gather.6
  86.0 55.0 all-gather.10
  143.8 125.7 all-gather.8
  272.3 75.6 all-gather.12
  350.7 76.0 all-gather.14
  484.1 177.4 reduce-scatter.5
  664.4 180.6 reduce-scatter.13
  847.9 184.4 reduce-scatter.11
  1035.2 144.4 reduce-scatter.9
  1186.2 152.1 reduce-scatter.7
where the time goes:
time: 1350 us
  waiting for transfers between devices  860 us (64%)
  matrix products  239 us (18%)
  blocking collectives  127 us (9%)
  other arithmetic  52.5 us (4%)
  local copies, waits for them, and re-layouts  51.3 us (4%)
  between operations  15.3 us (1%)
    reduce_scatter x1, waiting for transfers between devices, body(): lax.psum_scatter(grad_weight_in, ('dp', 'ctx'), scatter_dimension=0, tile...  187 us
    reduce_scatter x1, waiting for transfers between devices, body(): lax.psum_scatter(grad_weight_qkv, ('dp', 'ctx'), scatter_dimension=0, til...  159 us
    reduce_scatter x1, waiting for transfers between devices, body(): lax.psum_scatter(grad_weight_out, ('dp', 'ctx'), scatter_dimension=0, til...  147 us
    all_gather x1, waiting for transfers between devices, body(): lax.all_gather(key_value, 'ctx', axis=0, tiled=True)  126 us
    reduce_scatter x1, waiting for transfers between devices, body(): lax.psum_scatter(grad_weight_fc2, ('dp', 'ctx'), scatter_dimension=0, til...  104 us
    unnamed x2, blocking collectives  88.6 us
    reduce_scatter x1, waiting for transfers between devices, body(): lax.psum_scatter(grad_pairs.astype(jnp.bfloat16), 'ctx', scatter_dimensio...  72.1 us
    dot_general x1, matrix products, body(): jnp.einsum('qhd,khd->hqk', grad_attended, values, preferred_element_type=...  42.4 us
  transfers between devices with their start and end apart: 10, of which 8 were waited for; matrix products, arithmetic and copies ran while one was open for 25% of the time, Pallas kernels for 0%

commit v1 on v0

v1 whole, which is shorter than its diff:
```python
import functools

import jax
import jax.numpy as jnp
from jax import lax
from jax.experimental import pallas as pl
from jax.experimental.pallas import tpu as pltpu
from jax.sharding import Mesh
from jax.sharding import PartitionSpec as P

HEAD = 64
ROT = 16
LONGEST = 2048
GROUP_IN = 4
TILE = 256
EPS = 1e-05
NEG = -1e30
F32 = jnp.float32
BF16 = jnp.bfloat16
G_AXES = ("dp", "out")
ALL_AXES = ("dp", "out", "in")


def dot(a, b):
    return jnp.dot(a, b, preferred_element_type=F32)


def dot_nt(a, b):
    return lax.dot_general(a, b, (((1,), (1,)), ((), ())), preferred_element_type=F32)


def dot_tn(a, b):
    return lax.dot_general(a, b, (((0,), (0,)), ((), ())), preferred_element_type=F32)


def xor_swap(value, axis, size, step):
    return lax.ppermute(value, axis, [(i, i ^ step) for i in range(size)])


def rotary(x, cos, sin_l, sin_r, sign):
    left = pltpu.roll(x, 128 - ROT // 2, 1)
    right = pltpu.roll(x, ROT // 2, 1)
    return x * cos - sign * (left * sin_l) + sign * (right * sin_r)


def prep_kernel(heads, z_ref, n1_ref, dy_ref, w_ref, wo_ref, b_ref, cos_ref, sl_ref, sr_ref, qk_ref, vdo_ref):
    z = z_ref[0]
    joined = dot(n1_ref[...], w_ref[...]) + b_ref[...]
    grad_att = dot_nt(dy_ref[...], wo_ref[...])
    cos, sl, sr = cos_ref[...], sl_ref[...], sr_ref[...]
    base = heads * 128
    for h in range(heads):
        part = joined[:, h * 128 : (h + 1) * 128]
        qk_ref[z ^ h] = rotary(part, cos, sl, sr, 1.0).astype(BF16)
        vdo_ref[z ^ h] = jnp.concatenate(
            [joined[:, base + h * HEAD : base + (h + 1) * HEAD], grad_att[:, h * HEAD : (h + 1) * HEAD]], axis=1
        ).astype(BF16)


def prep(z, n1, dy, w, wo, bias, cos, sl, sr):
    rows, width = n1.shape
    heads = w.shape[1] // (3 * HEAD)
    row = lambda i, z: (i, 0)
    whole = lambda i, z: (0, 0)
    out = jax.ShapeDtypeStruct((heads, rows, 2 * HEAD), BF16)
    out_spec = pl.BlockSpec((heads, TILE, 2 * HEAD), lambda i, z: (0, i, 0))
    return pl.pallas_call(
        functools.partial(prep_kernel, heads),
        grid_spec=pltpu.PrefetchScalarGridSpec(
            num_scalar_prefetch=1,
            grid=(rows // TILE,),
            in_specs=[
                pl.BlockSpec((TILE, width), row),
                pl.BlockSpec((TILE, width), row),
                pl.BlockSpec(w.shape, whole),
                pl.BlockSpec(wo.shape, whole),
                pl.BlockSpec(bias.shape, whole),
                pl.BlockSpec((TILE, 2 * HEAD), row),
                pl.BlockSpec((TILE, 2 * HEAD), row),
                pl.BlockSpec((TILE, 2 * HEAD), row),
            ],
            out_specs=[out_spec, out_spec],
        ),
        out_shape=[out, out],
        compiler_params=pltpu.CompilerParams(vmem_limit_bytes=40 * 2**20),
        cost_estimate=pl.CostEstimate(flops=2 * rows * width * 1024, bytes_accessed=12 * 2**20, transcendentals=0),
    )(z, n1, dy, w, wo, bias, cos, sl, sr)


def post_kernel(heads, z_ref, dqk_ref, dvo_ref, cos_ref, sl_ref, sr_ref, da_ref, o_ref):
    z = z_ref[0]
    cos, sl, sr = cos_ref[...], sl_ref[...], sr_ref[...]
    base = heads * 128
    for h in range(heads):
        part = dqk_ref[z ^ h].astype(F32)
        da_ref[:, h * 128 : (h + 1) * 128] = rotary(part, cos, sl, sr, -1.0).astype(BF16)
    for h in range(0, heads, 2):
        one, two = dvo_ref[z ^ h].astype(F32), dvo_ref[z ^ (h + 1)].astype(F32)
        da_ref[:, base + h * HEAD : base + (h + 2) * HEAD] = jnp.concatenate(
            [one[:, :HEAD], two[:, :HEAD]], axis=1
        ).astype(BF16)
        o_ref[:, h * HEAD : (h + 2) * HEAD] = jnp.concatenate([one[:, HEAD:], two[:, HEAD:]], axis=1).astype(BF16)


def post(z, dqk, dvo, cos, sl, sr):
    heads, rows, _ = dqk.shape
    row = lambda i, z: (i, 0)
    slab = pl.BlockSpec((heads, TILE, 2 * HEAD), lambda i, z: (0, i, 0))
    table = pl.BlockSpec((TILE, 2 * HEAD), row)
    return pl.pallas_call(
        functools.partial(post_kernel, heads),
        grid_spec=pltpu.PrefetchScalarGridSpec(
            num_scalar_prefetch=1,
            grid=(rows // TILE,),
            in_specs=[slab, slab, table, table, table],
            out_specs=[pl.BlockSpec((TILE, heads * 3 * HEAD), row), pl.BlockSpec((TILE, heads * HEAD), row)],
        ),
        out_shape=[
            jax.ShapeDtypeStruct((rows, heads * 3 * HEAD), BF16),
            jax.ShapeDtypeStruct((rows, heads * HEAD), BF16),
        ],
        compiler_params=pltpu.CompilerParams(vmem_limit_bytes=40 * 2**20),
        cost_estimate=pl.CostEstimate(flops=rows * 2048, bytes_accessed=5 * 2**20, transcendentals=0),
    )(z, dqk, dvo, cos, sl, sr)


def doc_start(packed, ends_ref, count):
    start = packed * 0
    for d in range(count):
        start = jnp.where(packed >= ends_ref[d], ends_ref[d], start)
    return start


def doc_end(packed, ends_ref, count):
    end = ends_ref[count - 1]
    for d in range(count - 2, -1, -1):
        end = jnp.where(packed < ends_ref[d], ends_ref[d], end)
    return end


def attend_kernel(
    block, count, source_ref, ends_ref, qk_ref, vdo_ref, dqk_ref, dvo_ref, q_s, k_s, v_s, do_s, qk_t, vdo_t, dq_t, lse_s, delta_s, o_s
):
    rows = qk_ref.shape[0]
    tiles = rows // TILE
    per = TILE // block
    scale = HEAD ** (-0.5)

    def gather(i, carry):
        at = pl.multiple_of(i * TILE, TILE)
        for b in range(per):
            src = pl.multiple_of(source_ref[i * per + b] * block, block)
            dst = pl.multiple_of(at + b * block, block)
            qk = qk_ref[pl.ds(src, block), :].astype(F32)
            vdo = vdo_ref[pl.ds(src, block), :].astype(F32)
            q_s[pl.ds(dst, block), :] = (qk[:, :HEAD] * scale).astype(BF16)
            k_s[pl.ds(dst, block), :] = qk[:, HEAD:].astype(BF16)
            v_s[pl.ds(dst, block), :] = vdo[:, :HEAD].astype(BF16)
            do_s[pl.ds(dst, block), :] = vdo[:, HEAD:].astype(BF16)
        here = pl.ds(at, TILE)
        qk_t[:HEAD, here] = q_s[here, :].astype(F32).T.astype(BF16)
        qk_t[HEAD:, here] = k_s[here, :].astype(F32).T.astype(BF16)
        vdo_t[:HEAD, here] = v_s[here, :].astype(F32).T.astype(BF16)
        vdo_t[HEAD:, here] = do_s[here, :].astype(F32).T.astype(BF16)
        dq_t[:, here] = jnp.zeros((HEAD, TILE), F32)
        return carry

    lax.fori_loop(0, tiles, gather, 0)

    key_at = lax.broadcasted_iota(jnp.int32, (TILE, TILE), 0)
    query_at = lax.broadcasted_iota(jnp.int32, (TILE, TILE), 1)

    def scores(i, j):
        s = dot(k_s[pl.ds(pl.multiple_of(j * TILE, TILE), TILE), :], qk_t[:HEAD, pl.ds(pl.multiple_of(i * TILE, TILE), TILE)])
        query_row = i * TILE + lax.broadcasted_iota(jnp.int32, (1, TILE), 1)
        first = doc_start(query_row, ends_ref, count) - j * TILE
        last = (i - j) * TILE + query_at
        return jnp.where((key_at >= first) & (key_at <= last), s, NEG)

    def forward(i, carry):
        here = pl.ds(pl.multiple_of(i * TILE, TILE), TILE)

        def step(j, state):
            top, total, acc = state
            s = scores(i, j)
            new_top = jnp.maximum(top, jnp.max(s, axis=0, keepdims=True))
            p = jnp.exp(s - new_top)
            fade = jnp.exp(top - new_top)
            total = total * fade + jnp.sum(p, axis=0, keepdims=True)
            acc = acc * fade + dot(vdo_t[:HEAD, pl.ds(pl.multiple_of(j * TILE, TILE), TILE)], p.astype(BF16))
            return new_top, total, acc

        low = doc_start(i * TILE, ends_ref, count) // TILE
        top, total, acc = lax.fori_loop(
            low, i + 1, step, (jnp.full((1, TILE), NEG, F32), jnp.zeros((1, TILE), F32), jnp.zeros((HEAD, TILE), F32))
        )
        out = acc / total
        lse_s[:, here] = top + jnp.log(total)
        delta_s[:, here] = jnp.sum(out * vdo_t[HEAD:, here].astype(F32), axis=0, keepdims=True)
        o_s[here, :] = out.T.astype(BF16)
        return carry

    lax.fori_loop(0, tiles, forward, 0)

    def backward(j, carry):
        keys = pl.ds(pl.multiple_of(j * TILE, TILE), TILE)

        def step(i, state):
            dk, dv = state
            here = pl.ds(pl.multiple_of(i * TILE, TILE), TILE)
            p = jnp.exp(scores(i, j) - lse_s[:, here])
            dp = dot(v_s[keys, :], vdo_t[HEAD:, here])
            ds = (p * (dp - delta_s[:, here])).astype(BF16)
            dv = dv + dot(p.astype(BF16), do_s[here, :])
            dk = dk + dot(ds, q_s[here, :])
            dq_t[:, here] += dot(qk_t[HEAD:, keys], ds)
            return dk, dv

        high = (doc_end(j * TILE + TILE - 1, ends_ref, count) - 1) // TILE
        zero = jnp.zeros((TILE, HEAD), F32)
        dk, dv = lax.fori_loop(j, high + 1, step, (zero, zero))
        k_s[keys, :] = dk.astype(BF16)
        v_s[keys, :] = dv.astype(BF16)
        return carry

    lax.fori_loop(0, tiles, backward, 0)

    def scatter(i, carry):
        at = pl.multiple_of(i * TILE, TILE)
        here = pl.ds(at, TILE)
        dq = (dq_t[:, here] * scale).T
        dqk = jnp.concatenate([dq, k_s[here, :].astype(F32)], axis=1).astype(BF16)
        dvo = jnp.concatenate([v_s[here, :].astype(F32), o_s[here, :].astype(F32)], axis=1).astype(BF16)
        for b in range(per):
            dst = pl.ds(pl.multiple_of(source_ref[i * per + b] * block, block), block)
            dqk_ref[dst, :] = dqk[b * block : (b + 1) * block, :]
            dvo_ref[dst, :] = dvo[b * block : (b + 1) * block, :]
        return carry

    lax.fori_loop(0, tiles, scatter, 0)


def attend(source, ends, qk, vdo, block):
    rows, lanes = qk.shape
    out = jax.ShapeDtypeStruct((rows, lanes), BF16)
    in_vmem = pl.BlockSpec(memory_space=pltpu.VMEM)
    in_smem = pl.BlockSpec(memory_space=pltpu.SMEM)
    half = pltpu.VMEM((rows, HEAD), BF16)
    turned = pltpu.VMEM((lanes, rows), BF16)
    return pl.pallas_call(
        functools.partial(attend_kernel, block, ends.shape[0]),
        in_specs=[in_smem, in_smem, in_vmem, in_vmem],
        out_specs=[in_vmem, in_vmem],
        out_shape=[out, out],
        scratch_shapes=[
            half,
            half,
            half,
            half,
            turned,
            turned,
            pltpu.VMEM((HEAD, rows), F32),
            pltpu.VMEM((1, rows), F32),
            pltpu.VMEM((1, rows), F32),
            half,
        ],
        compiler_params=pltpu.CompilerParams(vmem_limit_bytes=40 * 2**20),
        cost_estimate=pl.CostEstimate(
            flops=rows * rows * HEAD * 8, bytes_accessed=4 * rows * lanes * 2, transcendentals=rows * rows
        ),
    )(source, ends, qk, vdo)


def gather_in(value):
    far = jnp.stack([value, xor_swap(value, "in", GROUP_IN, 2)])
    near = xor_swap(far, "in", GROUP_IN, 1)
    return jnp.stack([far[0], near[0], far[1], near[1]])


def scatter_in(parts):
    near = xor_swap(jnp.stack([parts[1], parts[3]]).astype(BF16), "in", GROUP_IN, 1)
    far = xor_swap((parts[2] + near[1].astype(F32)).astype(BF16), "in", GROUP_IN, 2)
    return parts[0] + near[0].astype(F32) + far.astype(F32)


def exchange_in(parts, t):
    here = [lax.dynamic_index_in_dim(parts, t ^ s, 0, keepdims=False) for s in range(GROUP_IN)]
    there = [here[0]] + [xor_swap(here[s], "in", GROUP_IN, s) for s in range(1, GROUP_IN)]
    stacked = jnp.stack(there)
    return jnp.stack([lax.dynamic_index_in_dim(stacked, t ^ u, 0, keepdims=False) for u in range(GROUP_IN)])


def exchange_out(parts, size):
    return jnp.stack([parts[0]] + [xor_swap(parts[s], "out", size, s) for s in range(1, size)])


def body(
    tokens,
    seq_lengths,
    dealing,
    ln1_gain,
    ln1_bias,
    ln2_gain,
    ln2_bias,
    w_qkv,
    b_qkv,
    w_out,
    w_in,
    b_in,
    w_fc2,
    b_out,
    cotangent,
):
    n_dp, n_out, n_in = lax.axis_size("dp"), lax.axis_size("out"), lax.axis_size("in")
    n_g = n_dp * n_out
    n_all = n_g * n_in
    rows_dev, width = tokens.shape
    ff = w_in.shape[1]
    r_w = w_in.shape[0]
    r_ff = w_fc2.shape[0]
    block = LONGEST // (2 * n_out * n_in)
    slots_dev = rows_dev // block
    heads = width // HEAD
    h_in = heads // n_in
    cols = h_in * HEAD
    rows = rows_dev * n_in
    z, t = lax.axis_index("out"), lax.axis_index("in")
    g = lax.axis_index("dp") * n_out + z
    z_arr = z[None].astype(jnp.int32)
    lengths, order = seq_lengths[0], dealing[0]
    n_seq = lengths.shape[0]
    ends = jnp.cumsum(lengths)

    slots = order.shape[0]
    packed_ids = jnp.arange(slots, dtype=jnp.int32)
    slot_of = jnp.sum(jnp.where(order[None, :] == packed_ids[:, None], packed_ids[None, :], 0), axis=1)
    chunk = slot_of // slots_dev
    source = (((chunk // n_in) ^ z) * n_in + ((chunk % n_in) ^ t)) * slots_dev + slot_of % slots_dev
    source = source.astype(jnp.int32)

    part = jnp.arange(rows, dtype=jnp.int32)
    place_slot = (z * n_in + ((part // rows_dev) ^ t)) * slots_dev + (part % rows_dev) // block
    picked = jnp.sum(jnp.where(place_slot[:, None] == packed_ids[None, :], order[None, :], 0), axis=1)
    packed = picked * block + part % block
    starts = jnp.max(jnp.where(packed[:, None] >= ends[None, :], ends[None, :], 0), axis=1)
    position = (packed - starts).astype(F32)
    lane = jnp.arange(2 * HEAD, dtype=jnp.int32) % HEAD
    half = ROT // 2
    freq = 10000.0 ** (-2.0 * (lane % half).astype(F32) / ROT)
    phase = position[:, None] * freq[None, :]
    cos = jnp.where(lane < ROT, jnp.cos(phase), 1.0)
    sine = jnp.sin(phase)
    sin_l = jnp.where(lane < half, sine, 0.0)
    sin_r = jnp.where((lane >= half) & (lane < ROT), sine, 0.0)

    vectors = [ln1_gain, ln1_bias, ln2_gain, ln2_bias, b_qkv, b_out, b_in]
    sizes = [v.shape[0] for v in vectors]
    n_vec = sum(sizes)
    qkv_cols = w_qkv.reshape(r_w, 3, n_in, h_in, HEAD)
    qk_cols = jnp.transpose(qkv_cols[:, :2], (2, 0, 3, 1, 4)).reshape(n_in, r_w, 2 * cols)
    v_cols = jnp.transpose(qkv_cols[:, 2], (1, 0, 2, 3)).reshape(n_in, r_w, cols)
    in_cols = jnp.transpose(w_in.reshape(r_w, n_g, n_in, r_ff), (2, 0, 1, 3)).reshape(n_in, r_w, ff // n_in)
    joined_cols = exchange_in(jnp.concatenate([qk_cols, v_cols, in_cols], axis=2), t).reshape(n_in * r_w, -1)
    vec_in = exchange_in(jnp.broadcast_to(jnp.concatenate(vectors)[None], (n_in, n_vec)), t).reshape(-1)
    vec_rows = -(-n_in * n_vec // width)
    vec_rows = -(-vec_rows // 16) * 16
    vec_in = jnp.pad(vec_in, (0, vec_rows * width - n_in * n_vec)).reshape(vec_rows, width)
    home = [(d, (d % n_g) * n_in + d // n_g) for d in range(n_all)]
    out_rows = lax.ppermute(w_out, ALL_AXES, home).reshape(n_in * r_w, cols)
    first = jnp.concatenate([jnp.concatenate([joined_cols[:, : 3 * cols], out_rows], axis=1), vec_in], axis=0)
    first = lax.all_gather(first, G_AXES, axis=0, tiled=False)
    second = jnp.concatenate([joined_cols[:, 3 * cols :], w_fc2], axis=1)
    second = lax.all_gather(second, G_AXES, axis=0, tiled=True)
    weight_qkv = first[:, : n_in * r_w, : 3 * cols].reshape(width, 3 * cols)
    weight_out = first[:, : n_in * r_w, 3 * cols :].reshape(cols, width)
    weight_in, weight_fc2 = second[:, : ff // n_in], second[:, ff // n_in :]
    vec_all = first[:, n_in * r_w :].reshape(n_g, -1)[:, : n_in * n_vec].reshape(n_g, n_in, n_vec).astype(F32)
    spans, at = [], 0
    for size in sizes:
        spans.append(vec_all[:, :, at : at + size])
        at += size
    gain_one, shift_one, gain_two, shift_two = [s.reshape(width) for s in spans[:4]]
    bias_out = spans[5].reshape(width)
    bias_in = lax.dynamic_index_in_dim(spans[6], t, 1, keepdims=False).reshape(ff // n_in)
    bias_qkv = lax.dynamic_index_in_dim(spans[4].reshape(3, n_in, h_in, HEAD), t, 1, keepdims=False)
    bias_qkv = jnp.concatenate([jnp.transpose(bias_qkv[:2], (1, 0, 2)).reshape(-1), bias_qkv[2].reshape(-1)])

    both = gather_in(jnp.concatenate([tokens, cotangent], axis=1))
    x_all = both[:, :, :width].reshape(rows, width).astype(F32)
    dy_all = both[:, :, width:].reshape(rows, width)
    centre = jnp.mean(x_all, axis=-1, keepdims=True)
    centred = x_all - centre
    rstd = lax.rsqrt(jnp.mean(centred * centred, axis=-1, keepdims=True) + EPS)
    xhat = centred * rstd
    n1 = (xhat * gain_one + shift_one).astype(BF16)
    n2 = (xhat * gain_two + shift_two).astype(BF16)

    qk, vdo = prep(z_arr, n1, dy_all, weight_qkv, weight_out, bias_qkv[None], cos, sin_l, sin_r)
    qk = exchange_out(qk, n_out).reshape(n_out * rows, 2 * HEAD)
    vdo = exchange_out(vdo, n_out).reshape(n_out * rows, 2 * HEAD)
    dqk, dvo = attend(source, ends, qk, vdo, block)
    dqk = exchange_out(dqk.reshape(n_out, rows, 2 * HEAD), n_out)
    dvo = exchange_out(dvo.reshape(n_out, rows, 2 * HEAD), n_out)
    da, o = post(z_arr, dqk, dvo, cos, sin_l, sin_r)

    up = dot(n2, weight_in) + bias_in
    hidden, back_gelu = jax.vjp(lambda v: jax.nn.gelu(v, approximate=False), up)
    hidden = hidden.astype(BF16)
    grad_up = back_gelu(dot_nt(dy_all, weight_fc2))[0].astype(BF16)
    grad_fc2 = dot_tn(hidden, dy_all)
    grad_in = dot_tn(n2, grad_up)
    grad_b_in = jnp.sum(grad_up.astype(F32), axis=0)
    dn2 = dot_nt(grad_up, weight_in)
    second_grads = jnp.concatenate([grad_in.astype(BF16), grad_fc2.astype(BF16)], axis=1)
    second_grads = lax.psum_scatter(second_grads, G_AXES, scatter_dimension=0, tiled=True)

    y_part = dot(hidden, weight_fc2) + dot(o, weight_out)
    own = tokens.astype(F32)
    mixed = (own + scatter_in(y_part.reshape(n_in, rows_dev, width)) + bias_out).astype(BF16)

    dn1 = dot_nt(da, weight_qkv)
    grad_qkv = dot_tn(n1, da)
    grad_out = dot_tn(o, dy_all)
    grad_b_qkv = jnp.sum(da.astype(F32), axis=0)

    def placed(vector, parts, axis):
        spread = jnp.expand_dims(vector, axis)
        mask = (jnp.arange(parts) == t).reshape([-1 if a == axis else 1 for a in range(spread.ndim)])
        return jnp.where(mask, spread, 0.0)

    qk_grad = jnp.transpose(grad_b_qkv[: 2 * cols].reshape(h_in, 2, HEAD), (1, 0, 2)).reshape(2, cols)
    b_qkv_grad = jnp.concatenate([qk_grad, grad_b_qkv[None, 2 * cols :]], axis=0)
    grad_own = cotangent.astype(F32)
    vec_grads = [
        jnp.sum(dn1 * xhat, axis=0),
        jnp.sum(dn1, axis=0),
        jnp.sum(dn2 * xhat, axis=0),
        jnp.sum(dn2, axis=0),
        placed(b_qkv_grad, n_in, 1).reshape(-1),
        jnp.sum(grad_own, axis=0),
        placed(grad_b_in.reshape(n_g, r_ff), n_in, 1).reshape(-1),
    ]
    vec_grads = jnp.concatenate([v.reshape(n_g, n_in, -1) for v in vec_grads], axis=2).reshape(n_g, -1)
    vec_grads = jnp.pad(vec_grads, ((0, 0), (0, vec_rows * width - n_in * n_vec))).reshape(n_g, vec_rows, width)
    first_grads = jnp.concatenate(
        [
            grad_qkv.astype(BF16).reshape(n_g, n_in * r_w, 3 * cols),
            grad_out.astype(BF16).reshape(n_g, n_in * r_w, cols),
        ],
        axis=2,
    )
    first_grads = jnp.concatenate([first_grads, vec_grads.astype(BF16)], axis=1)
    first_grads = lax.psum_scatter(first_grads, G_AXES, scatter_dimension=0, tiled=False)

    in_part = second_grads[:, : ff // n_in].reshape(n_in, r_w, ff // n_in)
    in_part = exchange_in(in_part, t).reshape(n_in, r_w, n_g, r_ff)
    grad_w_in = jnp.transpose(in_part, (1, 2, 0, 3)).reshape(r_w, ff).astype(F32)
    grad_w_fc2 = second_grads[:, ff // n_in :].astype(F32)
    qkv_part = exchange_in(first_grads[: n_in * r_w, : 3 * cols].reshape(n_in, r_w, 3 * cols), t)
    qk_part = jnp.transpose(qkv_part[:, :, : 2 * cols].reshape(n_in, r_w, h_in, 2, HEAD), (1, 3, 0, 2, 4))
    v_part = jnp.transpose(qkv_part[:, :, 2 * cols :], (1, 0, 2)).reshape(r_w, width)
    grad_w_qkv = jnp.concatenate([qk_part.reshape(r_w, 2 * width), v_part], axis=1).astype(F32)
    back_home = [(b, a) for a, b in home]
    out_part = first_grads[: n_in * r_w, 3 * cols :].reshape(r_w, width)
    grad_w_out = lax.ppermute(out_part, ALL_AXES, back_home).astype(F32)
    vec_part = first_grads[n_in * r_w :].reshape(-1)[: n_in * n_vec].reshape(n_in, n_vec)
    vec_part = jnp.sum(exchange_in(vec_part, t).astype(F32), axis=0)
    vec_out, at = [], 0
    for size in sizes:
        vec_out.append(vec_part[at : at + size])
        at += size

    w_sum = scatter_in((gain_one * dn1 + gain_two * dn2).reshape(n_in, rows_dev, width))
    own_hat, own_rstd = xhat[:rows_dev], rstd[:rows_dev]
    mean_w = jnp.mean(w_sum, axis=-1, keepdims=True)
    mean_wx = jnp.mean(w_sum * own_hat, axis=-1, keepdims=True)
    grad_tokens = grad_own + own_rstd * (w_sum - mean_w - own_hat * mean_wx)
    return (
        mixed,
        grad_tokens,
        vec_out[0],
        vec_out[1],
        vec_out[2],
        vec_out[3],
        grad_w_qkv,
        vec_out[4],
        grad_w_out,
        grad_w_in,
        vec_out[6],
        grad_w_fc2,
        vec_out[5],
    )


def solution(mesh):
    n_dp, n_ctx = mesh.shape["dp"], mesh.shape["ctx"]
    split = Mesh(mesh.devices.reshape(n_dp, n_ctx // GROUP_IN, GROUP_IN), ALL_AXES)
    mat, vec, group = P(ALL_AXES, None), P(ALL_AXES), P("dp", None)
    return jax.shard_map(
        body,
        mesh=split,
        in_specs=(mat, group, group, vec, vec, vec, vec, mat, vec, mat, mat, vec, mat, vec, mat),
        out_specs=(mat, mat, vec, vec, vec, vec, mat, vec, mat, mat, vec, mat, vec),
        check_vma=False,
    )
```

time: 1350 us -> 529 us (0.39)
  waiting for transfers between devices: 860 us -> 255 us
  matrix products: 239 us -> 45.7 us
  blocking collectives: 127 us -> 0 us
  Pallas kernels: 0 us -> 69.2 us
  starting transfers between devices: 0.4 us -> 55.2 us
  other arithmetic: 52.5 us -> 38.8 us
    reduce_scatter x5 -> x2, waiting for transfers between devices: 669 us -> 91.9 us  [the longest x1 81.1 us: body(): lax.psum_scatter(second_grads, G_AXES, scatter_dimension=0, tiled=True)]
    dot_general x18 -> x10, matrix products: 239 us -> 45.7 us  [the longest x3 21.5 us: dot(): return jnp.dot(a, b, preferred_element_type=F32)]
    all_gather x5 -> x2, waiting for transfers between devices: 188 us -> 16.9 us  [the longest x1 16.9 us: body(): first = lax.all_gather(first, G_AXES, axis=0, tiled=False)]
    ppermute x0 -> x35, waiting for transfers between devices: none -> 146 us  [the longest x33 146 us: xor_swap(): return lax.ppermute(value, axis, [(i, i ^ step) for i in range(size)])]
    unnamed x2 -> x0, blocking collectives: 88.6 us -> none
    pallas_call x0 -> x3, Pallas kernels: none -> 69.2 us  [the longest x1 64.2 us: attend(): pl.pallas_call(functools.partial(attend_kernel, block, ends.shape[0]), in...]
    ppermute x0 -> x35, starting transfers between devices: none -> 54.6 us  [the longest x33 53.3 us: xor_swap(): return lax.ppermute(value, axis, [(i, i ^ step) for i in range(size)])]
    all_gather x1 -> x0, blocking collectives: 38.8 us -> none  [body(): lax.all_gather(b_in, ('dp', 'ctx'), axis=0, tiled=True)]
  transfers between devices with their start and end apart: 10 -> 39, of which waited for: 8 -> 19; matrix products, arithmetic and copies ran while one was open for 25% -> 16% of each run, Pallas kernels for 0% -> 13%
where the time goes in v1:
time: 529 us; the launch traced here: 526 us
  waiting for transfers between devices  255 us (48%)
  Pallas kernels  69.2 us (13%)
  starting transfers between devices  55.2 us (10%)
  local copies, waits for them, and re-layouts  46.5 us (9%)
  matrix products  45.7 us (9%)
  other arithmetic  38.8 us (7%)
  between operations  15.3 us (3%)
    ppermute x33, waiting for transfers between devices, xor_swap(): return lax.ppermute(value, axis, [(i, i ^ step) for i in range(size)])  146 us
    reduce_scatter x1, waiting for transfers between devices, body(): lax.psum_scatter(second_grads, G_AXES, scatter_dimension=0, tiled=True)  81.1 us
    pallas_call x1, Pallas kernels, attend(): pl.pallas_call(functools.partial(attend_kernel, block, ends.shape[0]), in...  64.2 us
    ppermute x33, starting transfers between devices, xor_swap(): return lax.ppermute(value, axis, [(i, i ^ step) for i in range(size)])  53.3 us
    dot_general x3, matrix products, dot(): return jnp.dot(a, b, preferred_element_type=F32)  21.5 us
    unnamed x66, local copies, waits for them, and re-layouts  18.2 us
    all_gather x1, waiting for transfers between devices, body(): first = lax.all_gather(first, G_AXES, axis=0, tiled=False)  16.9 us
    dot_general x4, matrix products, dot_tn(): lax.dot_general(a, b, (((0,), (0,)), ((), ())), preferred_element_type=F32)  13.1 us
  transfers between devices with their start and end apart: 39, of which 19 were waited for; matrix products, arithmetic and copies ran while one was open for 16% of the time, Pallas kernels for 13%

profile of v1, /device:TPU:0, one launch (start us, length us, event | category | flops | bytes accessed | tf_op | source)
XLA Modules:
  0.0 525.6 jit_solution(16954579703749625032)
XLA Ops:
  7.2 4.8 concatenate.43
  27.1 4.2 collective-permute-start
  31.3 22.0 %collective-permute-done = bf16[256,2048]{1,0:T(8,128)(2,1)S(1)} collective-permute-done((bf16[256,2048]{1,0:T(8,128)(2,1)S(1)}, bf16[256,2048]{1,0:T(8,128)(2,1)S(1)}, u32[]{:S(2)}, u32[]{:S(2)}) %collective-permute-start) | collective-permute-done | bytes 1048608 | tf_op jit(solution)/shard_map/ppermute | solution.py:37
  67.7 16.9 %all-gather.6.cloned.1.call-done = bf16[1152,1024]{1,0:T(8,128)(2,1)} async-done(((bf16[144,1024]{1,0:T(8,128)(2,1)}), bf16[1152,1024]{1,0:T(8,128)(2,1)}) %all-gather.6.cloned.1.call-update) | async-done | bytes 2359312 | tf_op jit(solution)/shard_map/all_gather | solution.py:371
  92.2 5.4 %add_convert_fusion.1 = (bf16[1024,1024]{1,0:T(8,128)(2,1)S(1)}, f32[1024,1024]{1,0:T(8,128)}) fusion(f32[1024]{0:T(1024)S(1)} %add.267, f32[1024]{0:T(1024)S(1)} %mul.158, f32[1024]{0:T(1024)S(1)} %bitcast.224, f32[1024]{0:T(1024)S(1)} %bitcast.225, f32[4,256,1024]{2,1,0:T(8,128)} %get-tuple-element.108), kind=kLoop, calls=%fused_computation.11 | loop fusion | flops 5242880 | bytes 10502144 | tf_op jit(solution)/shard_map/convert_element_type | solution.py:395
  108.1 17.0 %collective-permute-done.12 = bf16[1024,128]{1,0:T(8,128)(2,1)S(1)} collective-permute-done((bf16[1024,128]{1,0:T(8,128)(2,1)S(1)}, bf16[1024,128]{1,0:T(8,128)(2,1)S(1)}, u32[]{:S(2)}, u32[]{:S(2)}) %collective-permute-start.12) | collective-permute-done | bytes 262176 | tf_op jit(solution)/shard_map/ppermute | solution.py:37
  125.1 7.2 %collective-permute-start.11 = (bf16[1024,128]{1,0:T(8,128)(2,1)S(1)}, bf16[1024,128]{1,0:T(8,128)(2,1)S(1)}, u32[]{:S(2)}, u32[]{:S(2)}) collective-permute-start(bf16[1024,128]{1,0:T(8,128)(2,1)S(1)} %get-tuple-element.128), channel_id=1, source_target_pairs={{0,12},{4,8},{8,4},{12,0},{1,13},{5,9},{9,5},{13,1},{2,14},{6,10},... | collective-permute-start | bytes 786440 | tf_op jit(solution)/shard_map/ppermute | solution.py:37
  133.3 8.3 %collective-permute-done.9 = bf16[1024,128]{1,0:T(8,128)(2,1)S(1)} collective-permute-done((bf16[1024,128]{1,0:T(8,128)(2,1)S(1)}, bf16[1024,128]{1,0:T(8,128)(2,1)S(1)}, u32[]{:S(2)}, u32[]{:S(2)}) %collective-permute-start.9) | collective-permute-done | bytes 262176 | tf_op jit(solution)/shard_map/ppermute | solution.py:37
  141.6 34.8 %collective-permute-done.10 = bf16[1024,128]{1,0:T(8,128)(2,1)S(1)} collective-permute-done((bf16[1024,128]{1,0:T(8,128)(2,1)S(1)}, bf16[1024,128]{1,0:T(8,128)(2,1)S(1)}, u32[]{:S(2)}, u32[]{:S(2)}) %collective-permute-start.10) | collective-permute-done | bytes 262176 | tf_op jit(solution)/shard_map/ppermute | solution.py:37
  176.5 64.2 %shard_map.247 = (bf16[4096,128]{1,0:T(8,128)(2,1)S(1)}, bf16[4096,128]{1,0:T(8,128)(2,1)S(1)}) custom-call(s32[64]{0:T(128)S(1)} %fusion.52.source_ref, s32[4]{0:T(128)S(1)} %bitcast.184, bf16[4096,128]{1,0:T(8,128)(2,1)S(1)} %bitcast.182, bf16[4096,128]{1,0:T(8,128)(2,1)S(1)} %bitcast.181), custom_call_target="tpu_custom_call" | custom-call | flops 8589934592 | bytes 4194304 | tf_op jit(solution)/shard_map/pallas_call | solution.py:250
  241.5 15.4 %collective-permute-start.18 = (bf16[1024,128]{1,0:T(8,128)(2,1)S(1)}, bf16[1024,128]{1,0:T(8,128)(2,1)}, u32[]{:S(2)}, u32[]{:S(2)}) collective-permute-start(bf16[1024,128]{1,0:T(8,128)(2,1)S(1)} %get-tuple-element.118), channel_id=1, source_target_pairs={{0,4},{4,0},{8,12},{12,8},{1,5},{5,1},{9,13},{13,9},{2,6},{6,2},{1... | collective-permute-start | bytes 786440 | tf_op jit(solution)/shard_map/ppermute | solution.py:37
  262.1 8.0 %collective-permute-done.18 = bf16[1024,128]{1,0:T(8,128)(2,1)} collective-permute-done((bf16[1024,128]{1,0:T(8,128)(2,1)S(1)}, bf16[1024,128]{1,0:T(8,128)(2,1)}, u32[]{:S(2)}, u32[]{:S(2)}) %collective-permute-start.18) | collective-permute-done | bytes 262176 | tf_op jit(solution)/shard_map/ppermute | solution.py:37
  270.4 8.2 %collective-permute-done.19 = bf16[1024,128]{1,0:T(8,128)(2,1)} collective-permute-done((bf16[1024,128]{1,0:T(8,128)(2,1)}, bf16[1024,128]{1,0:T(8,128)(2,1)}, u32[]{:S(2)}, u32[]{:S(2)}) %collective-permute-start.19) | collective-permute-done | bytes 262176 | tf_op jit(solution)/shard_map/ppermute | solution.py:37
  280.6 19.5 %collective-permute-done.16 = bf16[1024,128]{1,0:T(8,128)(2,1)} collective-permute-done((bf16[1024,128]{1,0:T(8,128)(2,1)}, bf16[1024,128]{1,0:T(8,128)(2,1)}, u32[]{:S(2)}, u32[]{:S(2)}) %collective-permute-start.16) | collective-permute-done | bytes 262176 | tf_op jit(solution)/shard_map/ppermute | solution.py:37
  311.5 5.1 convolution_convert_fusion.2
  316.6 14.8 %multiply_convert_fusion = (bf16[1024,1024]{1,0:T(8,128)(2,1)}, f32[1024,1024]{1,0:T(8,128)S(1)}, f32[1024,1024]{1,0:T(8,128)S(1)}) fusion(f32[1024]{0:T(1024)S(1)} %bitcast.228, bf16[1024,2048]{1,0:T(8,128)(2,1)} %all-gather.4.cloned.1.call-done, f32[1024,1024]{1,0:T(8,128)} %get-tuple-element.102, f32[1024]{0:T(1024)S(1)} %add.257, f32[1024]{0:T(1024)S(1)} %mul.150), kind=kOutput, calls=%fused_computation.12 | convolution fusion | flops 2219835392 | bytes 16789504 | tf_op jit(solution)/shard_map/dot_general | solution.py:25
  331.4 4.1 convert_reduce_fusion
  339.4 4.6 fusion.62
  348.4 4.1 convolution_convert_fusion
  357.4 6.5 %copy.98 = bf16[1024,2048]{1,0:T(8,128)(2,1)} copy(bf16[1024,2048]{0,1:T(8,128)(2,1)} %pad_maximum_fusion.1) | data formatting | bytes 8388608
  379.9 11.1 %collective-permute-done.24 = bf16[256,1024]{1,0:T(8,128)(2,1)S(1)} collective-permute-done((bf16[256,1024]{1,0:T(8,128)(2,1)}, bf16[256,1024]{1,0:T(8,128)(2,1)S(1)}, u32[]{:S(2)}, u32[]{:S(2)}) %collective-permute-start.24) | collective-permute-done | bytes 524320 | tf_op jit(solution)/shard_map/ppermute | solution.py:37
  392.8 8.9 %collective-permute-done.22 = bf16[256,1024]{1,0:T(8,128)(2,1)S(1)} collective-permute-done((bf16[256,1024]{1,0:T(8,128)(2,1)S(1)}, bf16[256,1024]{1,0:T(8,128)(2,1)S(1)}, u32[]{:S(2)}, u32[]{:S(2)}) %collective-permute-start.22) | collective-permute-done | bytes 524320 | tf_op jit(solution)/shard_map/ppermute | solution.py:37
  407.1 10.8 %reduce-scatter.5.cloned.1.call-done = bf16[1,144,1024]{2,1,0:T(8,128)(2,1)} async-done(((bf16[8,144,1024]{2,1,0:T(8,128)(2,1)}), bf16[1,144,1024]{2,1,0:T(8,128)(2,1)}) %reduce-scatter.5.cloned.1.call-update) | async-done | bytes 294928 | tf_op jit(solution)/shard_map/reduce_scatter | solution.py:453
  429.1 81.1 %reduce-scatter.7.cloned.1.call-done = bf16[128,2048]{1,0:T(8,128)(2,1)} async-done(((bf16[1024,2048]{1,0:T(8,128)(2,1)}), bf16[128,2048]{1,0:T(8,128)(2,1)}) %reduce-scatter.7.cloned.1.call-update) | async-done | bytes 524304 | tf_op jit(solution)/shard_map/reduce_scatter | solution.py:415
  (293 shorter events, 123.6 us)
Async XLA Ops:
  7.2 77.4 %all-gather.6.cloned.1.call-start = ((), (), s32[]{:S(2)}) async-start(), calls=%async_computation.4 | async-start | bytes 2654208 | tf_op jit(solution)/shard_map/all_gather | solution.py:371
  12.0 8.4 %collective-permute-start.6 = (bf16[384]{0:T(512)(128)(2,1)S(1)}, bf16[384]{0:T(512)(128)(2,1)S(1)}, u32[]{:S(2)}, u32[]{:S(2)}) collective-permute-start(bf16[384]{0:T(512)(128)(2,1)S(1)} %concatenate.43), channel_id=1, source_target_pairs={{0,1},{1,0},{2,3},{3,2},{4,5},{5,4},{6,7},{7,6},{8,9},{9,8},{10,11... | collective-permute-start | bytes 2312 | tf_op jit(solution)/shard_map/ppermute | solution.py:37
  12.4 8.3 %collective-permute-start.7 = (bf16[384]{0:T(512)(128)(2,1)S(1)}, bf16[384]{0:T(512)(128)(2,1)S(1)}, u32[]{:S(2)}, u32[]{:S(2)}) collective-permute-start(bf16[384]{0:T(512)(128)(2,1)S(1)} %concatenate.43), channel_id=1, source_target_pairs={{0,2},{1,3},{2,0},{3,1},{4,6},{5,7},{6,4},{7,5},{8,10},{9,11},{10,... | collective-permute-start | bytes 2312 | tf_op jit(solution)/shard_map/ppermute | solution.py:37
  26.9 289.8 %all-gather.4.cloned.1.call-start = ((), (), s32[]{:S(2)}) async-start(), calls=%async_computation.2 | async-start | bytes 4718592 | tf_op jit(solution)/shard_map/all_gather | solution.py:373
  27.1 26.2 %collective-permute-start = (bf16[256,2048]{1,0:T(8,128)(2,1)S(1)}, bf16[256,2048]{1,0:T(8,128)(2,1)S(1)}, u32[]{:S(2)}, u32[]{:S(2)}) collective-permute-start(bf16[256,2048]{1,0:T(8,128)(2,1)S(1)} %get-tuple-element.134), channel_id=1, source_target_pairs={{0,2},{1,3},{2,0},{3,1},{4,6},{5,7},{6,4},{7,5},{8,10},{9,11},{10,... | collective-permute-start | bytes 3145736 | tf_op jit(solution)/shard_map/ppermute | solution.py:37
  54.8 6.8 %collective-permute-start.1 = (bf16[2,256,2048]{2,1,0:T(8,128)(2,1)}, bf16[2,256,2048]{2,1,0:T(8,128)(2,1)}, u32[]{:S(2)}, u32[]{:S(2)}) collective-permute-start(bf16[2,256,2048]{2,1,0:T(8,128)(2,1)} %pad_maximum_fusion.3), channel_id=1, source_target_pairs={{0,1},{1,0},{2,3},{3,2},{4,5},{5,4},{6,7},{7,6},{8,9},{9,8},{10,11... | collective-permute-start | bytes 6291464 | tf_op jit(solution)/shard_map/ppermute | solution.py:37
  61.4 356.5 %reduce-scatter.5.cloned.1.call-start = ((), (), s32[]{:S(2)}) async-start(), calls=%async_computation.3 | async-start | bytes 2654208 | tf_op jit(solution)/shard_map/reduce_scatter | solution.py:453
  101.2 23.9 %collective-permute-start.12 = (bf16[1024,128]{1,0:T(8,128)(2,1)S(1)}, bf16[1024,128]{1,0:T(8,128)(2,1)S(1)}, u32[]{:S(2)}, u32[]{:S(2)}) collective-permute-start(bf16[1024,128]{1,0:T(8,128)(2,1)S(1)} %get-tuple-element.126), channel_id=1, source_target_pairs={{0,4},{4,0},{8,12},{12,8},{1,5},{5,1},{9,13},{13,9},{2,6},{6,2},{1... | collective-permute-start | bytes 786440 | tf_op jit(solution)/shard_map/ppermute | solution.py:37
  102.9 29.4 %collective-permute-start.13 = (bf16[1024,128]{1,0:T(8,128)(2,1)S(1)}, bf16[1024,128]{1,0:T(8,128)(2,1)S(1)}, u32[]{:S(2)}, u32[]{:S(2)}) collective-permute-start(bf16[1024,128]{1,0:T(8,128)(2,1)S(1)} %get-tuple-element.125), channel_id=1, source_target_pairs={{0,8},{4,12},{8,0},{12,4},{1,9},{5,13},{9,1},{13,5},{2,10},{6,14},... | collective-permute-start | bytes 786440 | tf_op jit(solution)/shard_map/ppermute | solution.py:37
  103.6 29.6 %collective-permute-start.14 = (bf16[1024,128]{1,0:T(8,128)(2,1)S(1)}, bf16[1024,128]{1,0:T(8,128)(2,1)S(1)}, u32[]{:S(2)}, u32[]{:S(2)}) collective-permute-start(bf16[1024,128]{1,0:T(8,128)(2,1)S(1)} %get-tuple-element.124), channel_id=1, source_target_pairs={{0,12},{4,8},{8,4},{12,0},{1,13},{5,9},{9,5},{13,1},{2,14},{6,10},... | collective-permute-start | bytes 786440 | tf_op jit(solution)/shard_map/ppermute | solution.py:37
  105.9 35.7 %collective-permute-start.9 = (bf16[1024,128]{1,0:T(8,128)(2,1)S(1)}, bf16[1024,128]{1,0:T(8,128)(2,1)S(1)}, u32[]{:S(2)}, u32[]{:S(2)}) collective-permute-start(bf16[1024,128]{1,0:T(8,128)(2,1)S(1)} %get-tuple-element.130), channel_id=1, source_target_pairs={{0,4},{4,0},{8,12},{12,8},{1,5},{5,1},{9,13},{13,9},{2,6},{6,2},{1... | collective-permute-start | bytes 786440 | tf_op jit(solution)/shard_map/ppermute | solution.py:37
  106.6 69.7 %collective-permute-start.10 = (bf16[1024,128]{1,0:T(8,128)(2,1)S(1)}, bf16[1024,128]{1,0:T(8,128)(2,1)S(1)}, u32[]{:S(2)}, u32[]{:S(2)}) collective-permute-start(bf16[1024,128]{1,0:T(8,128)(2,1)S(1)} %get-tuple-element.129), channel_id=1, source_target_pairs={{0,8},{4,12},{8,0},{12,4},{1,9},{5,13},{9,1},{13,5},{2,10},{6,14},... | collective-permute-start | bytes 786440 | tf_op jit(solution)/shard_map/ppermute | solution.py:37
  125.1 51.2 %collective-permute-start.11 = (bf16[1024,128]{1,0:T(8,128)(2,1)S(1)}, bf16[1024,128]{1,0:T(8,128)(2,1)S(1)}, u32[]{:S(2)}, u32[]{:S(2)}) collective-permute-start(bf16[1024,128]{1,0:T(8,128)(2,1)S(1)} %get-tuple-element.128), channel_id=1, source_target_pairs={{0,12},{4,8},{8,4},{12,0},{1,13},{5,9},{9,5},{13,1},{2,14},{6,10},... | collective-permute-start | bytes 786440 | tf_op jit(solution)/shard_map/ppermute | solution.py:37
  241.5 28.6 %collective-permute-start.18 = (bf16[1024,128]{1,0:T(8,128)(2,1)S(1)}, bf16[1024,128]{1,0:T(8,128)(2,1)}, u32[]{:S(2)}, u32[]{:S(2)}) collective-permute-start(bf16[1024,128]{1,0:T(8,128)(2,1)S(1)} %get-tuple-element.118), channel_id=1, source_target_pairs={{0,4},{4,0},{8,12},{12,8},{1,5},{5,1},{9,13},{13,9},{2,6},{6,2},{1... | collective-permute-start | bytes 786440 | tf_op jit(solution)/shard_map/ppermute | solution.py:37
  256.9 21.7 %collective-permute-start.19 = (bf16[1024,128]{1,0:T(8,128)(2,1)}, bf16[1024,128]{1,0:T(8,128)(2,1)}, u32[]{:S(2)}, u32[]{:S(2)}) collective-permute-start(bf16[1024,128]{1,0:T(8,128)(2,1)} %get-tuple-element.117), channel_id=1, source_target_pairs={{0,8},{4,12},{8,0},{12,4},{1,9},{5,13},{9,1},{13,5},{2,10},{6,14},... | collective-permute-start | bytes 786440 | tf_op jit(solution)/shard_map/ppermute | solution.py:37
  256.9 21.7 %collective-permute-start.20 = (bf16[1024,128]{1,0:T(8,128)(2,1)S(1)}, bf16[1024,128]{1,0:T(8,128)(2,1)}, u32[]{:S(2)}, u32[]{:S(2)}) collective-permute-start(bf16[1024,128]{1,0:T(8,128)(2,1)S(1)} %get-tuple-element.116), channel_id=1, source_target_pairs={{0,12},{4,8},{8,4},{12,0},{1,13},{5,9},{9,5},{13,1},{2,14},{6,10},... | collective-permute-start | bytes 786440 | tf_op jit(solution)/shard_map/ppermute | solution.py:37
  260.1 20.5 %collective-permute-start.15 = (bf16[1024,128]{1,0:T(8,128)(2,1)}, bf16[1024,128]{1,0:T(8,128)(2,1)}, u32[]{:S(2)}, u32[]{:S(2)}) collective-permute-start(bf16[1024,128]{1,0:T(8,128)(2,1)} %get-tuple-element.122), channel_id=1, source_target_pairs={{0,4},{4,0},{8,12},{12,8},{1,5},{5,1},{9,13},{13,9},{2,6},{6,2},{1... | collective-permute-start | bytes 786440 | tf_op jit(solution)/shard_map/ppermute | solution.py:37
  261.2 38.8 %collective-permute-start.16 = (bf16[1024,128]{1,0:T(8,128)(2,1)}, bf16[1024,128]{1,0:T(8,128)(2,1)}, u32[]{:S(2)}, u32[]{:S(2)}) collective-permute-start(bf16[1024,128]{1,0:T(8,128)(2,1)} %get-tuple-element.121), channel_id=1, source_target_pairs={{0,8},{4,12},{8,0},{12,4},{1,9},{5,13},{9,1},{13,5},{2,10},{6,14},... | collective-permute-start | bytes 786440 | tf_op jit(solution)/shard_map/ppermute | solution.py:37
  270.1 30.0 %collective-permute-start.17 = (bf16[1024,128]{1,0:T(8,128)(2,1)}, bf16[1024,128]{1,0:T(8,128)(2,1)}, u32[]{:S(2)}, u32[]{:S(2)}) collective-permute-start(bf16[1024,128]{1,0:T(8,128)(2,1)} %get-tuple-element.120), channel_id=1, source_target_pairs={{0,12},{4,8},{8,4},{12,0},{1,13},{5,9},{9,5},{13,1},{2,14},{6,10},... | collective-permute-start | bytes 786440 | tf_op jit(solution)/shard_map/ppermute | solution.py:37
  348.1 162.2 %reduce-scatter.7.cloned.1.call-start = ((), (), s32[]{:S(2)}) async-start(), calls=%async_computation.5 | async-start | bytes 4718592 | tf_op jit(solution)/shard_map/reduce_scatter | solution.py:415
  365.7 8.1 %collective-permute-start.23 = (bf16[2,256,1024]{2,1,0:T(8,128)(2,1)S(1)}, bf16[2,256,1024]{2,1,0:T(8,128)(2,1)S(1)}, u32[]{:S(2)}, u32[]{:S(2)}) collective-permute-start(bf16[2,256,1024]{2,1,0:T(8,128)(2,1)S(1)} %pad_maximum_fusion.9), channel_id=1, source_target_pairs={{0,1},{1,0},{2,3},{3,2},{4,5},{5,4},{6,7},{7,6},{8,9},{9,8},{10,11... | collective-permute-start | bytes 3145736 | tf_op jit(solution)/shard_map/ppermute | solution.py:37
  376.0 14.9 %collective-permute-start.24 = (bf16[256,1024]{1,0:T(8,128)(2,1)}, bf16[256,1024]{1,0:T(8,128)(2,1)S(1)}, u32[]{:S(2)}, u32[]{:S(2)}) collective-permute-start(bf16[256,1024]{1,0:T(8,128)(2,1)} %fusion.18), channel_id=1, source_target_pairs={{0,2},{1,3},{2,0},{3,1},{4,6},{5,7},{6,4},{7,5},{8,10},{9,11},{10,... | collective-permute-start | bytes 1572872 | tf_op jit(solution)/shard_map/ppermute | solution.py:37
  379.4 22.3 %collective-permute-start.22 = (bf16[256,1024]{1,0:T(8,128)(2,1)S(1)}, bf16[256,1024]{1,0:T(8,128)(2,1)S(1)}, u32[]{:S(2)}, u32[]{:S(2)}) collective-permute-start(bf16[256,1024]{1,0:T(8,128)(2,1)S(1)} %fusion.20), channel_id=1, source_target_pairs={{0,2},{1,3},{2,0},{3,1},{4,6},{5,7},{6,4},{7,5},{8,10},{9,11},{10,... | collective-permute-start | bytes 1572872 | tf_op jit(solution)/shard_map/ppermute | solution.py:37
  424.5 89.6 %collective-permute-start.31 = (bf16[32,1024]{1,0:T(8,128)(2,1)S(1)}, bf16[32,1024]{1,0:T(8,128)(2,1)S(1)}, u32[]{:S(2)}, u32[]{:S(2)}) collective-permute-start(bf16[32,1024]{1,0:T(8,128)(2,1)S(1)} %reshape.427), channel_id=1, source_target_pairs={{0,0},{4,1},{8,2},{12,3},{16,4},{20,5},{24,6},{28,7},{1,8},{5,9},{... | collective-permute-start | bytes 196616 | tf_op jit(solution)/shard_map/ppermute | solution.py:465
  (41 other events, 351.5 us)
Sparse Core Ops, SparseCore 0:
  27.0 57.5 all-gather.5
  87.2 106.7 all-gather.3
  348.2 69.6 reduce-scatter.4
  421.4 88.8 reduce-scatter.6
